TPU v7x, 32 devices: a whole 2x2x4 slice. The times are simulated.
32 devices in a mesh: cls: 4 (over z), ptl: 8 (over y, x, core).
Axes of the slice: x: 2, y: 2, z: 4, core: 2. Of those that a mesh axis runs over, the one named last changes fastest.
Arguments:
- particles: bfloat16 [16384, 64, 128], P(('cls', 'ptl')), may hold values from -6 to 6
- references: bfloat16 [64, 200, 128], P('ptl', 'cls'), may hold values from -0.029907227 to 0.029907227
- best_class: int32 [16384], P(('cls', 'ptl')), may hold values from 0 to 199, as said below
- best_turn: int32 [16384], P(('cls', 'ptl')), may hold values from 0 to 35
Outputs:
- best_score: float32 [16384], P(('cls', 'ptl'))
- new_references: float32 [64, 200, 128], P('ptl', 'cls')
Inputs may be any that keep to these rules, and one draw needn't show every extreme that they name: `best_class`: in each aligned block of 512 rows (the particles of one device), at most 160 classes lie in one class shard, classes k * 50 to (k + 1) * 50 - 1; some class shard receives exactly 160 from every block.
All inputs are finite; a program needn't handle non-finite values.
Results may differ from a plain program's by a relative error of at most 0.0048.
Values may be sent and summed in bfloat16 or wider, within the bound.
A program may use at most 192 MiB of HBM per device.

v0:
```python
import math

import jax
import jax.numpy as jnp
from jax import lax
from jax.sharding import PartitionSpec as P

ROTS = 36
C_DEV = 50
SLOT_CAP = 160


def spectrum_table(angles, freq_count):
    position = jnp.arange(angles, dtype=jnp.int32)
    freq_index = jnp.arange(freq_count, dtype=jnp.int32)
    phases = (
        2.0
        * math.pi
        / angles
        * (position[:, None] * freq_index[None, :] % angles).astype(jnp.float32)
    )
    factor = 1.0 / math.sqrt(angles)
    return (jnp.concatenate([jnp.cos(phases), -jnp.sin(phases)], axis=1) * factor).astype(
        jnp.bfloat16
    )


def rotation_table(freq_count, turns):
    freq_index = jnp.arange(freq_count, dtype=jnp.int32)
    turn_index = jnp.arange(turns, dtype=jnp.int32)
    phases = (
        2.0
        * math.pi
        / turns
        * (freq_index[:, None] * turn_index[None, :] % turns).astype(jnp.float32)
    )
    weight = jnp.where(freq_index == 0, 1.0, 2.0).astype(jnp.float32)[:, None]
    return jnp.stack([weight * jnp.cos(phases), -weight * jnp.sin(phases)]).astype(jnp.bfloat16)


def quarter(panel):
    half_width = panel.shape[-1] // 2
    return jnp.concatenate([panel[..., half_width:], -panel[..., :half_width]], axis=-1)


def rotate_back(spectra, turn_of, turns):
    freq_count = spectra.shape[0]
    half_width = spectra.shape[-1] // 2
    freq_index = jnp.arange(freq_count, dtype=jnp.int32)
    phases = (
        2.0 * math.pi / turns * (freq_index[:, None] * turn_of[None, :] % turns).astype(jnp.float32)
    )
    cosine = jnp.cos(phases)[:, :, None]
    sine_part = jnp.sin(phases)[:, :, None]
    real_part = spectra[..., :half_width].astype(jnp.float32)
    imag_part = spectra[..., half_width:].astype(jnp.float32)
    return jnp.concatenate(
        [real_part * cosine + imag_part * sine_part, imag_part * cosine - real_part * sine_part],
        axis=-1,
    ).astype(jnp.bfloat16)


def polar_spectra(particles, freq_count):
    count_p, cycle_count, angles = particles.shape
    dft_table = spectrum_table(angles, freq_count)
    raw_terms = jnp.einsum("ipa,ak->kip", particles, dft_table, preferred_element_type=jnp.float32)
    spectra = raw_terms.astype(jnp.bfloat16).reshape(2, freq_count, count_p, cycle_count)
    return jnp.transpose(spectra, (1, 2, 0, 3)).reshape(freq_count, count_p, 2 * cycle_count)


def local(particles, references, best_class, best_turn):
    count_p, cycle_count, angles = particles.shape
    freq_count = angles // 2
    spectra = polar_spectra(particles, freq_count)
    turn_table = rotation_table(freq_count, ROTS)
    all_freqs = lax.all_gather(references, "ptl", axis=0, tiled=True)
    group_size = min(count_p, 128)
    panel_part = lax.all_gather(all_freqs, "cls", axis=1, tiled=True)
    class_width = panel_part.shape[1]
    stacked = jnp.concatenate([panel_part, quarter(panel_part)], axis=1)
    maxima = []
    for offset in range(0, count_p, group_size):
        group_rows = spectra[:, offset : offset + group_size]
        cross_terms = jnp.einsum(
            "mik,mck->mic", group_rows, stacked, preferred_element_type=jnp.float32
        ).astype(jnp.bfloat16)
        cross_terms = cross_terms.reshape(freq_count, group_size, 2, class_width)
        scores = jnp.einsum(
            "mijc,jmr->irc", cross_terms, turn_table, preferred_element_type=jnp.float32
        )
        maxima.append(jnp.max(scores, axis=(1, 2)))
    best_score = jnp.concatenate(maxima)
    aligned = rotate_back(spectra, best_turn, ROTS)
    owners = lax.axis_size("cls")
    peer_count = lax.axis_size("ptl")
    slot_cap = SLOT_CAP
    owner_of = best_class // C_DEV
    local_class = best_class - owner_of * C_DEV
    owner_hits = (owner_of[:, None] == jnp.arange(owners, dtype=jnp.int32)[None, :]).astype(
        jnp.int32
    )
    slot_rank = jnp.sum((jnp.cumsum(owner_hits, axis=0) - owner_hits) * owner_hits, axis=1)
    slot_index = owner_of * slot_cap + slot_rank
    outgoing = jnp.zeros((freq_count, owners * slot_cap, 2 * cycle_count), jnp.bfloat16)
    outgoing = (
        outgoing.at[:, slot_index, :]
        .set(aligned)
        .reshape(freq_count, owners, slot_cap, 2 * cycle_count)
    )
    labels = (
        jnp.full((owners * slot_cap,), -1.0, jnp.bfloat16)
        .at[slot_index]
        .set(local_class.astype(jnp.bfloat16))
    )
    labels = jnp.broadcast_to(labels.reshape(1, owners, slot_cap), (peer_count, owners, slot_cap))
    arrived, arrived_labels = (
        lax.all_to_all(
            lax.all_to_all(outgoing, "cls", split_axis=1, concat_axis=1, tiled=True),
            "ptl",
            split_axis=0,
            concat_axis=2,
            tiled=True,
        ),
        lax.all_to_all(
            lax.all_to_all(labels, "cls", split_axis=1, concat_axis=1, tiled=True),
            "ptl",
            split_axis=0,
            concat_axis=2,
            tiled=True,
        ),
    )
    arrived_rows = arrived.reshape(arrived.shape[0], -1, 2 * cycle_count)
    class_marks = jnp.arange(C_DEV, dtype=jnp.float32).astype(jnp.bfloat16)
    member = (arrived_labels.reshape(1, -1) == class_marks[:, None]).astype(jnp.bfloat16)
    totals = jnp.einsum("cs,msk->mck", member, arrived_rows, preferred_element_type=jnp.float32)
    counts = jnp.sum(member.astype(jnp.float32), axis=1)
    new_references = totals / (counts + 1.0)[None, :, None]
    return (best_score, new_references)


def solution(mesh):
    return jax.shard_map(
        local,
        mesh=mesh,
        in_specs=(
            P(("cls", "ptl"), None, None),
            P("ptl", "cls", None),
            P(("cls", "ptl")),
            P(("cls", "ptl")),
        ),
        out_specs=(P(("cls", "ptl")), P("ptl", "cls", None)),
        check_vma=False,
    )
```

profile of v0, /device:TPU:0, one launch (start us, length us, event | category | flops | bytes accessed | tf_op | source)
XLA Modules:
  0.0 620.9 jit_solution(3257332240550867480)
XLA Ops:
  7.2 0.7 subtract_convert_fusion
  7.9 1.2 reduce-window.6
  9.1 0.2 slice_reduce_fusion
  9.3 0.2 reduce-window.9
  9.5 0.1 add_bitcast_fusion
  9.6 3.8 scatter_custom_fusion.1
  13.4 0.1 broadcast_in_dim.23
  13.5 0.6 broadcast_in_dim.44
  14.1 6.5 %all-to-all-start.2 = ((bf16[8,4,160]{2,0,1:T(8,128)(2,1)}), bf16[8,4,160]{2,0,1:T(8,128)(2,1)S(1)}, u32[]{:S(2)}, u32[]{:S(2)}) async-start(bf16[8,4,160]{2,0,1:T(8,128)(2,1)} %broadcast_in_dim.44), calls=%async_computation.2 | async-start | bytes 32768 | tf_op jit(solution)/shard_map/all_to_all | solution.py:125
  20.6 0.1 sine_negate_fusion
  20.8 25.2 %fusion.6 = bf16[128,512,64]{1,0,2:T(8,128)(2,1)} fusion(bf16[512,64,128]{2,1,0:T(8,128)(2,1)} %param.4, f32[128,64]{0,1:T(8,128)S(1)} %get-tuple-element.18, f32[128,64]{0,1:T(8,128)S(1)} %get-tuple-element.19), kind=kOutput, calls=%fused_computation.17 | convolution fusion | flops 1077985280 | bytes 16842752 | tf_op jit(solution)/shard_map/ipa,ak->kip/dot_general | solution.py:66
  46.0 11.4 %copy.50 = bf16[2,64,512,64]{2,3,0,1:T(8,128)(2,1)} copy(bf16[2,64,512,64]{2,1,0,3:T(8,128)(2,1)} %bitcast.76) | data formatting | bytes 16777216 | tf_op jit(solution)/shard_map/reshape | solution.py:67
  57.4 0.5 fusion.37
  57.9 7.7 %fusion.1 = (bf16[64,512,64]{1,2,0:T(8,128)(2,1)}, bf16[64,512,64]{1,2,0:T(8,128)(2,1)}) fusion(f32[64,512]{1,0:T(8,128)S(1)} %get-tuple-element.17, f32[64,512]{1,0:T(8,128)S(1)} %get-tuple-element.16, bf16[64,512,128]{1,2,0:T(8,128)(2,1)} %bitcast.69), kind=kLoop, calls=%fused_computation.7 | loop fusion | flops 20971520 | bytes 17039360 | tf_op jit(solution)/shard_map/convert
  65.6 7.7 %maximum_bitcast_fusion = bf16[512,64,128]{0,2,1:T(8,128)(2,1)} fusion(bf16[64,512,64]{1,2,0:T(8,128)(2,1)} %get-tuple-element.13, bf16[64,512,64]{1,2,0:T(8,128)(2,1)} %get-tuple-element.12), kind=kLoop, calls=%fused_computation.10 | loop fusion | flops 16777216 | bytes 16777216 | tf_op jit(solution)/shard_map/concatenate | solution.py:57
  73.3 12.0 %copy.62 = bf16[512,64,128]{2,1,0:T(8,128)(2,1)} copy(bf16[512,64,128]{0,2,1:T(8,128)(2,1)} %maximum_bitcast_fusion) | data formatting | bytes 16777216 | tf_op jit(solution)/shard_map/concatenate | solution.py:57
  85.3 6.7 %broadcast_in_dim.20 = bf16[64,640,128]{2,0,1:T(8,128)(2,1)} broadcast(bf16[]{:T(256)} %constant.66.clone.1), dimensions={} | broadcast | bytes 10485762 | tf_op jit(solution)/shard_map/broadcast_in_dim | solution.py:104
  92.0 66.4 %scatter_fusion = bf16[64,640,128]{2,0,1:T(8,128)(2,1)} fusion(bf16[64,640,128]{2,0,1:T(8,128)(2,1)} %broadcast_in_dim.20, s32[512]{0:T(512)S(1)} %compare_select_fusion, bf16[512,64,128]{2,1,0:T(8,128)(2,1)} %copy.62), kind=kCustom, calls=%fused_computation | custom fusion | bytes 25167872 | tf_op jit(solution)/shard_map/scatter | solution.py:107
  158.4 14.6 %copy.63 = bf16[64,4,160,128]{3,2,0,1:T(8,128)(2,1)} copy(bf16[64,4,160,128]{3,0,2,1:T(8,128)(2,1)} %bitcast.67) | data formatting | bytes 20971520 | tf_op jit(solution)/shard_map/reshape | solution.py:108
  172.9 6.1 all-to-all-start
  179.0 0.0 all-gather.2.cloned.1.call-start
  179.1 11.9 %all_gather.6 = bf16[64,50,128]{2,0,1:T(8,128)(2,1)} all-gather(bf16[8,50,128]{2,0,1:T(8,128)(2,1)S(1)} %copy-done), channel_id=1, replica_groups=mesh['cls'=4,'ptl'=8] {'ptl'}, dimensions={0}, use_global_device_ids=true | all-gather | bytes 921600 | tf_op jit(solution)/shard_map/all_gather | solution.py:76
  191.0 0.0 all-gather.2.cloned.1.call-update
  191.1 0.6 copy.66
  191.7 268.1 %all-to-all-done = bf16[64,4,160,128]{3,2,0,1:T(8,128)(2,1)} async-done(((bf16[64,4,160,128]{3,2,0,1:T(8,128)(2,1)}), bf16[64,4,160,128]{3,2,0,1:T(8,128)(2,1)}, u32[]{:S(2)}, u32[]{:S(2)}) %all-to-all-start) | async-done | bytes 10485792 | tf_op jit(solution)/shard_map/all_to_all | solution.py:118
  459.8 3.7 all-to-all-start.3
  463.5 11.1 %copy.64 = bf16[64,4,160,128]{3,2,1,0:T(8,128)(2,1)} copy(bf16[64,4,160,128]{3,2,0,1:T(8,128)(2,1)} %all-to-all-done) | data formatting | bytes 20971520 | tf_op jit(solution)/shard_map/all_to_all | solution.py:118
  474.5 0.0 all-to-all-done.3
  474.5 5.1 all-to-all-start.1
  479.7 0.1 multiply_convert_fusion
  479.9 0.1 eq.68
  479.9 0.3 convert_reduce_fusion
  480.3 0.0 all-gather.2.cloned.1.call-done
  480.3 4.2 copy.54
  484.5 3.0 fusion.65
  487.5 7.1 %convolution_convert_fusion.3 = bf16[64,128,400]{1,2,0:T(8,128)(2,1)} fusion(bf16[64,512,128]{1,2,0:T(8,128)(2,1)S(1)} %bitcast.72, bf16[64,200,64]{2,1,0:T(8,128)(2,1)} %get-tuple-element.15, bf16[64,200,64]{2,1,0:T(8,128)(2,1)S(1)} %get-tuple-element.14, bf16[64,200,128]{2,1,0:T(8,128)(2,1)S(1)} %copy.54), kind=kOutput, calls=%fused_computation.16 | convolution fusion | flops 861798400 | bytes 16842752 | tf_op jit(solution)/shard_map/mik,mck->mic/dot_general | solution.py:84
  494.6 4.5 bitcast_reduce_fusion.3
  499.0 7.1 %convolution_convert_fusion.2 = bf16[64,128,400]{1,2,0:T(8,128)(2,1)} fusion(bf16[64,512,128]{1,2,0:T(8,128)(2,1)S(1)} %bitcast.73, bf16[64,200,64]{2,1,0:T(8,128)(2,1)} %get-tuple-element.15, bf16[64,200,64]{2,1,0:T(8,128)(2,1)S(1)} %get-tuple-element.14, bf16[64,200,128]{2,1,0:T(8,128)(2,1)S(1)} %copy.54), kind=kOutput, calls=%fused_computation.15 | convolution fusion | flops 861798400 | bytes 16842752 | tf_op jit(solution)/shard_map/mik,mck->mic/dot_general | solution.py:84
  506.1 4.5 bitcast_reduce_fusion.2
  510.6 7.3 %convolution_convert_fusion.1 = bf16[64,128,400]{1,2,0:T(8,128)(2,1)} fusion(bf16[64,512,128]{1,2,0:T(8,128)(2,1)S(1)} %bitcast.74, bf16[64,200,64]{2,1,0:T(8,128)(2,1)} %get-tuple-element.15, bf16[64,200,64]{2,1,0:T(8,128)(2,1)S(1)} %get-tuple-element.14, bf16[64,200,128]{2,1,0:T(8,128)(2,1)S(1)} %copy.54), kind=kOutput, calls=%fused_computation.14 | convolution fusion | flops 861798400 | bytes 16842752 | tf_op jit(solution)/shard_map/mik,mck->mic/dot_general | solution.py:84
  517.9 4.5 bitcast_reduce_fusion.1
  522.4 7.1 %convolution_convert_fusion = bf16[64,128,400]{1,2,0:T(8,128)(2,1)} fusion(bf16[64,512,128]{1,2,0:T(8,128)(2,1)S(1)} %bitcast.75, bf16[64,200,64]{2,1,0:T(8,128)(2,1)} %get-tuple-element.15, bf16[64,200,64]{2,1,0:T(8,128)(2,1)S(1)} %get-tuple-element.14, bf16[64,200,128]{2,1,0:T(8,128)(2,1)S(1)} %copy.54), kind=kOutput, calls=%fused_computation.13 | convolution fusion | flops 861798400 | bytes 16842752 | tf_op jit(solution)/shard_map/mik,mck->mic/dot_general | solution.py:84
  529.5 4.5 bitcast_reduce_fusion
  534.0 0.6 pad_maximum_fusion
  534.5 61.7 %all-to-all-done.1 = bf16[64,4,160,128]{3,2,1,0:T(8,128)(2,1)} async-done(((bf16[64,4,160,128]{3,2,1,0:T(8,128)(2,1)}), bf16[64,4,160,128]{3,2,1,0:T(8,128)(2,1)}, u32[]{:S(2)}, u32[]{:S(2)}) %all-to-all-start.1) | async-done | bytes 10485792 | tf_op jit(solution)/shard_map/all_to_all | solution.py:117
  596.2 10.7 %copy.65 = bf16[8,4,8,160,128]{4,3,2,1,0:T(8,128)(2,1)} copy(bf16[8,4,8,160,128]{4,3,1,0,2:T(8,128)(2,1)} %bitcast.23) | data formatting | bytes 20971520 | tf_op jit(solution)/shard_map/all_to_all | solution.py:117
  606.9 6.0 fusion.29
  612.9 0.7 copy.68
  (18 shorter events, 0.1 us)
Async XLA Ops:
  14.1 158.8 %all-to-all-start.2 = ((bf16[8,4,160]{2,0,1:T(8,128)(2,1)}), bf16[8,4,160]{2,0,1:T(8,128)(2,1)S(1)}, u32[]{:S(2)}, u32[]{:S(2)}) async-start(bf16[8,4,160]{2,0,1:T(8,128)(2,1)} %broadcast_in_dim.44), calls=%async_computation.2 | async-start | bytes 32768 | tf_op jit(solution)/shard_map/all_to_all | solution.py:125
  46.0 11.4 %copy-start.1 = (s32[512]{0:T(512)S(1)}, s32[512]{0:T(512)}, u32[]{:S(2)}) copy-start(s32[512]{0:T(512)} %param.7) | copy-start | bytes 6148
  172.9 6.2 copy-start
  172.9 286.9 %all-to-all-start = ((bf16[64,4,160,128]{3,2,0,1:T(8,128)(2,1)}), bf16[64,4,160,128]{3,2,0,1:T(8,128)(2,1)}, u32[]{:S(2)}, u32[]{:S(2)}) async-start(bf16[64,4,160,128]{3,2,0,1:T(8,128)(2,1)} %copy.63), calls=%async_computation | async-start | bytes 20971520 | tf_op jit(solution)/shard_map/all_to_all | solution.py:118
  179.0 301.2 %all-gather.2.cloned.1.call-start = ((), (), s32[]{:S(2)}) async-start(), calls=%async_computation.4 | async-start | bytes 4096000 | tf_op jit(solution)/shard_map/all_gather | solution.py:78
  459.8 14.7 %all-to-all-start.3 = ((bf16[8,4,160]{2,1,0:T(4,128)(2,1)}), bf16[8,4,160]{2,1,0:T(4,128)(2,1)S(1)}, u32[]{:S(2)}, u32[]{:S(2)}) async-start(bf16[8,4,160]{2,1,0:T(4,128)(2,1)} %copy.66), calls=%async_computation.3 | async-start | bytes 32768 | tf_op jit(solution)/shard_map/all_to_all | solution.py:124
  474.5 121.7 %all-to-all-start.1 = ((bf16[64,4,160,128]{3,2,1,0:T(8,128)(2,1)}), bf16[64,4,160,128]{3,2,1,0:T(8,128)(2,1)}, u32[]{:S(2)}, u32[]{:S(2)}) async-start(bf16[64,4,160,128]{3,2,1,0:T(8,128)(2,1)} %copy.64), calls=%async_computation.1 | async-start | bytes 20971520 | tf_op jit(solution)/shard_map/all_to_all | solution.py:117
  480.3 7.2 %slice-start = ((s8[8388608]{0:T(1024)(128)(4,1)}), s8[4194304]{0:T(1024)(128)(4,1)S(1)}, s32[]{:S(2)}) async-start(s8[8388608]{0:T(1024)(128)(4,1)} %bitcast.70), calls=%async_computation.5 | async-start | bytes 8388608
  484.5 3.0 slice-start.1
Sparse Core Ops, SparseCore 0:
  191.2 127.7 all-gather.1
where the time goes:
time: 626 us; the launch traced here: 621 us
  waiting for transfers between devices  330 us (53%)
  local copies, waits for them, and re-layouts  143 us (23%)
  matrix products  77.6 us (12%)
  other arithmetic  22.3 us (4%)
  starting transfers between devices  21.5 us (3%)
  between operations  14.6 us (2%)
  blocking collectives  11.9 us (2%)
    all_to_all x1, waiting for transfers between devices, local(): lax.all_to_all(outgoing, 'cls', split_axis=1, concat_axis=1, tiled=True)  268 us
    scatter x1, local copies, waits for them, and re-layouts, local(): outgoing = outgoing.at[:, slot_index, :].set(aligned).reshape(freq_count,...  66.4 us
    all_to_all x1, waiting for transfers between devices, local(): lax.all_to_all(lax.all_to_all(outgoing, 'cls', split_axis=1, concat_axis=...  61.7 us
    dot_general x4, matrix products, local(): jnp.einsum('mik,mck->mic', group_rows, stacked, preferred_element_type=jn...  28.5 us
    dot_general x1, matrix products, polar_spectra(): jnp.einsum('ipa,ak->kip', particles, dft_table, preferred_element_type=jn...  25.2 us
    dot_general x4, matrix products, local(): jnp.einsum('mijc,jmr->irc', cross_terms, turn_table, preferred_element_ty...  18 us
    reshape x1, local copies, waits for them, and re-layouts, local(): outgoing = outgoing.at[:, slot_index, :].set(aligned).reshape(freq_count,...  14.6 us
  transfers between devices with their start and end apart: 5, of which 2 were waited for; matrix products, arithmetic and copies ran while one was open for 35% of the time, Pallas kernels for 0%

commit v1 on v0

v1 whole, which is shorter than its diff:
```python
import functools
import math

import jax
import jax.numpy as jnp
import numpy as np
from jax import lax
from jax.experimental import pallas as pl
from jax.experimental.pallas import tpu as pltpu
from jax.sharding import PartitionSpec as P

ROTS = 36
LANES = 128
VMEM_LIMIT = 60 * 1024 * 1024
NT = (((1,), (1,)), ((), ()))


def fold_groups(freq_count, turns):
    groups = [[] for _ in range(turns // 2 + 1)]
    for m in range(freq_count):
        rest = m % turns
        if rest <= turns // 2:
            groups[rest].append((m, 1))
        else:
            groups[turns - rest].append((m, -1))
    return groups


def spectrum_table(angles, freq_count):
    position = jnp.arange(angles, dtype=jnp.int32)
    freq_index = jnp.arange(freq_count, dtype=jnp.int32)
    phases = (
        2.0
        * math.pi
        / angles
        * (position[:, None] * freq_index[None, :] % angles).astype(jnp.float32)
    )
    factor = 1.0 / math.sqrt(angles)
    return (jnp.concatenate([jnp.cos(phases), -jnp.sin(phases)], axis=1) * factor).astype(
        jnp.bfloat16
    )


def swap_halves(panel):
    half = panel.shape[-1] // 2
    return pltpu.roll(panel, half, panel.ndim - 1)


def spectra_kernel(
    groups,
    columns,
    step_pairs,
    class_count,
    table_ref,
    low_ref,
    high_ref,
    class_ref,
    cos_ref,
    sin_ref,
    spectra_out,
    sums_ref,
    raw_ref,
    held_ref,
    sem,
):
    step = pl.program_id(0)
    steps = pl.num_programs(0)
    freq_count = len(columns)
    half = LANES // 2
    table = table_ref[...]
    for pair in range(step_pairs):
        rows = jnp.concatenate([low_ref[pair], high_ref[pair]], axis=0)
        raw_ref[pl.ds(pair, 2 * freq_count, stride=step_pairs), :] = lax.dot_general(
            table, rows, NT, preferred_element_type=jnp.float32
        )
    first_half = lax.broadcasted_iota(jnp.int32, (step_pairs, LANES), 1) < half
    own_rows = pl.ds(pl.multiple_of(step * step_pairs, step_pairs), step_pairs)
    for m in range(freq_count):
        real = raw_ref[m * step_pairs : (m + 1) * step_pairs, :]
        imag = raw_ref[(freq_count + m) * step_pairs : (freq_count + m + 1) * step_pairs, :]
        at = slice(columns[m] * LANES, (columns[m] + 1) * LANES)
        held_ref[0, own_rows, at] = jnp.where(first_half, real, swap_halves(imag)).astype(
            jnp.bfloat16
        )
        held_ref[1, own_rows, at] = jnp.where(first_half, swap_halves(real), imag).astype(
            jnp.bfloat16
        )

    def write_back(at):
        rows = pl.ds(pl.multiple_of(at * step_pairs, step_pairs), step_pairs)
        return pltpu.make_async_copy(
            held_ref.at[:, rows, :], spectra_out.at[:, rows, :], sem.at[at]
        )

    write_back(step).start()

    @pl.when(step == steps - 1)
    def _():
        count_p = class_ref.shape[1]
        member = lax.broadcasted_iota(jnp.int32, (class_count, count_p), 0) == class_ref[...]
        lane = lax.broadcasted_iota(jnp.int32, (class_count, LANES), 1)
        flip = jnp.where(lane < half, 1.0, -1.0)
        column = 0
        for folded, group in enumerate(groups):
            width = len(group) * LANES
            at = slice(column, column + width)
            column += width
            weights = jnp.concatenate(
                [
                    jnp.where(member, cos_ref[folded : folded + 1, :], 0.0),
                    jnp.where(member, sin_ref[folded : folded + 1, :], 0.0),
                ],
                axis=0,
            ).astype(jnp.bfloat16)
            half_p = count_p // 2
            both = jnp.dot(
                weights[:, :half_p], held_ref[0, :, at], preferred_element_type=jnp.float32
            ) + jnp.dot(
                weights[:, half_p:], held_ref[1, :, at], preferred_element_type=jnp.float32
            )
            for place, (m, sign) in enumerate(group):
                part = both[:, place * LANES : (place + 1) * LANES]
                turned = swap_halves(part[class_count:]) * flip
                total = part[:class_count] + (turned if sign > 0 else -turned)
                sums_ref[m] = total.astype(jnp.bfloat16)
        for at in range(steps):
            write_back(at).wait()


def score_kernel(
    groups, cos_ref, sin_ref, panels_ref, spectra_ref, best_ref, stacked_ref, even_ref, odd_ref
):
    half = LANES // 2
    class_rows = panels_ref.shape[0]
    tiles = class_rows // 8
    last = len(groups) - 1

    @pl.when(pl.program_id(0) == 0)
    def _():
        lane = lax.broadcasted_iota(jnp.int32, (class_rows, LANES), 1)
        flip = jnp.where(lane < half, 1.0, -1.0)
        column = 0
        for group in groups:
            for m, sign in group:
                weight = 1.0 if m == 0 else 2.0
                panel = panels_ref[:, m * LANES : (m + 1) * LANES].astype(jnp.float32) * weight
                at = slice(column, column + LANES)
                column += LANES
                stacked_ref[0, :, at] = panel.astype(jnp.bfloat16)
                stacked_ref[1, :, at] = (swap_halves(panel) * (flip * sign)).astype(jnp.bfloat16)

    column = 0
    for folded, group in enumerate(groups):
        at = slice(column, column + len(group) * LANES)
        column += len(group) * LANES
        rows = spectra_ref[:, at]
        even = lax.dot_general(
            stacked_ref[0, :, at], rows, NT, preferred_element_type=jnp.float32
        )
        even_ref[:, folded * 8 : (folded + 1) * 8, :] = even.reshape(tiles, 8, -1)
        if 0 < folded < last:
            odd = lax.dot_general(
                stacked_ref[1, :, at], rows, NT, preferred_element_type=jnp.float32
            )
            odd_ref[:, (folded - 1) * 8 : folded * 8, :] = odd.reshape(tiles, 8, -1)

    width = spectra_ref.shape[0]
    cos_mat, sin_mat = cos_ref[...], sin_ref[...]

    def tile_step(tile, best):
        even = jnp.dot(
            cos_mat, even_ref[tile].astype(jnp.bfloat16), preferred_element_type=jnp.float32
        )
        odd = jnp.dot(
            sin_mat, odd_ref[tile].astype(jnp.bfloat16), preferred_element_type=jnp.float32
        )
        best = jnp.maximum(best, jnp.maximum(even[:8], even[last * 8 :]))
        for turn in range(1, last):
            best = jnp.maximum(
                best,
                even[turn * 8 : (turn + 1) * 8] + jnp.abs(odd[(turn - 1) * 8 : turn * 8]),
            )
        return best

    best = lax.fori_loop(0, tiles, tile_step, jnp.full((8, width), -jnp.inf, jnp.float32))
    best_ref[...] = jnp.max(best, axis=0, keepdims=True)


def local(particles, references, best_class, best_turn):
    count_p, cycle_count, angles = particles.shape
    freq_count = angles // 2
    groups = fold_groups(freq_count, ROTS)
    last = len(groups) - 1
    columns = [0] * freq_count
    place = 0
    for group in groups:
        for m, _ in group:
            columns[m] = place
            place += 1
    owners = lax.axis_size("cls")
    freqs_dev, classes_dev, _ = references.shape
    class_count = classes_dev * owners

    own = jnp.transpose(references, (1, 0, 2)).reshape(classes_dev, freqs_dev * LANES)
    panels = lax.all_gather(own, "cls", axis=0, tiled=True)
    panels = lax.all_gather(panels, "ptl", axis=1, tiled=True)
    all_labels = lax.all_gather(best_class, ("cls", "ptl"), axis=0, tiled=True)

    step_pairs = 32
    pairs = count_p // 2
    steps = pairs // step_pairs
    folded_index = jnp.arange(last + 1, dtype=jnp.int32)
    phases = (
        2.0
        * math.pi
        / ROTS
        * (folded_index[:, None] * best_turn[None, :] % ROTS).astype(jnp.float32)
    )
    table = spectrum_table(angles, freq_count).T
    whole = lambda *_: (0, 0)
    spectra, sums = pl.pallas_call(
        functools.partial(spectra_kernel, groups, columns, step_pairs, class_count),
        grid=(steps,),
        out_shape=(
            jax.ShapeDtypeStruct((2, pairs, freq_count * LANES), jnp.bfloat16),
            jax.ShapeDtypeStruct((freq_count, class_count, LANES), jnp.bfloat16),
        ),
        in_specs=[
            pl.BlockSpec((angles, 2 * freq_count), whole),
            pl.BlockSpec((step_pairs, cycle_count, angles), lambda g: (g, 0, 0)),
            pl.BlockSpec((step_pairs, cycle_count, angles), lambda g: (g + steps, 0, 0)),
            pl.BlockSpec((1, count_p), whole),
            pl.BlockSpec((last + 1, count_p), whole),
            pl.BlockSpec((last + 1, count_p), whole),
        ],
        out_specs=(
            pl.BlockSpec(memory_space=pl.ANY),
            pl.BlockSpec((freq_count, class_count, LANES), lambda g: (0, 0, 0)),
        ),
        scratch_shapes=[
            pltpu.VMEM((2 * freq_count * step_pairs, LANES), jnp.float32),
            pltpu.VMEM((2, pairs, freq_count * LANES), jnp.bfloat16),
            pltpu.SemaphoreType.DMA((steps,)),
        ],
        compiler_params=pltpu.CompilerParams(vmem_limit_bytes=VMEM_LIMIT),
        cost_estimate=pl.CostEstimate(
            flops=20_000_000_000, bytes_accessed=20_000_000, transcendentals=0
        ),
        name="spectra",
    )(
        table,
        particles,
        particles,
        best_class.reshape(1, count_p),
        jnp.cos(phases),
        jnp.sin(phases),
    )

    totals = lax.psum_scatter(sums, "ptl", scatter_dimension=0, tiled=True)
    totals = lax.psum_scatter(
        totals.reshape(freqs_dev, owners, classes_dev, LANES), "cls", scatter_dimension=1
    )

    turn_index = np.arange(last + 1)
    turn_phase = 2.0 * math.pi / ROTS * (turn_index[:, None] * turn_index[None, :] % ROTS)
    spread = np.eye(8, dtype=np.float32)
    cos_mat = jnp.asarray(np.kron(np.cos(turn_phase).astype(np.float32), spread), jnp.bfloat16)
    sin_mat = jnp.asarray(
        np.kron(-np.sin(turn_phase[1:last, 1:last]).astype(np.float32), spread), jnp.bfloat16
    )
    spectra = spectra.reshape(count_p, freq_count * LANES)
    block = 256
    best_score = pl.pallas_call(
        functools.partial(score_kernel, groups),
        grid=(count_p // block,),
        out_shape=jax.ShapeDtypeStruct((1, count_p), jnp.float32),
        in_specs=[
            pl.BlockSpec(cos_mat.shape, whole),
            pl.BlockSpec(sin_mat.shape, whole),
            pl.BlockSpec(panels.shape, whole, pipeline_mode=pl.Buffered(1)),
            pl.BlockSpec((block, freq_count * LANES), lambda g: (g, 0)),
        ],
        out_specs=pl.BlockSpec((1, block), lambda g: (0, g)),
        scratch_shapes=[
            pltpu.VMEM((2, class_count, freq_count * LANES), jnp.bfloat16),
            pltpu.VMEM((class_count // 8, 8 * (last + 1), block), jnp.float32),
            pltpu.VMEM((class_count // 8, 8 * (last - 1), block), jnp.float32),
        ],
        compiler_params=pltpu.CompilerParams(vmem_limit_bytes=VMEM_LIMIT),
        cost_estimate=pl.CostEstimate(
            flops=20_000_000_000, bytes_accessed=20_000_000, transcendentals=0
        ),
        name="score",
    )(cos_mat, sin_mat, panels, spectra)
    best_score = best_score.reshape(count_p)

    first_class = lax.axis_index("cls") * classes_dev
    own_classes = first_class + jnp.arange(classes_dev, dtype=jnp.int32)
    counts = jnp.sum((all_labels[None, :] == own_classes[:, None]).astype(jnp.float32), axis=1)
    new_references = totals.astype(jnp.float32) / (counts + 1.0)[None, :, None]
    return (best_score, new_references)


def solution(mesh):
    return jax.shard_map(
        local,
        mesh=mesh,
        in_specs=(
            P(("cls", "ptl"), None, None),
            P("ptl", "cls", None),
            P(("cls", "ptl")),
            P(("cls", "ptl")),
        ),
        out_specs=(P(("cls", "ptl")), P("ptl", "cls", None)),
        check_vma=False,
    )
```

time: 626 us -> 151 us (0.24)
  waiting for transfers between devices: 330 us -> 23.6 us
  local copies, waits for them, and re-layouts: 143 us -> 2.75 us
  matrix products: 77.6 us -> 0 us
  blocking collectives: 11.9 us -> 59.8 us
  Pallas kernels: 0 us -> 45.8 us
  starting transfers between devices: 21.5 us -> 0.12 us
  other arithmetic: 22.3 us -> 4.65 us
    all_to_all x4 -> x0, waiting for transfers between devices: 330 us -> none  [the longest x1 268 us: local(): lax.all_to_all(outgoing, 'cls', split_axis=1, concat_axis=1, tiled=True)]
    dot_general x10 -> x0, matrix products: 77.6 us -> none  [the longest x4 28.5 us: local(): jnp.einsum('mik,mck->mic', group_rows, stacked, preferred_element_type=jn...]
    scatter x2 -> x0, local copies, waits for them, and re-layouts: 70.1 us -> none  [the longest x1 66.4 us: local(): outgoing = outgoing.at[:, slot_index, :].set(aligned).reshape(freq_count,...]
    all_gather x1 -> x2, blocking collectives: 11.9 us -> 59.8 us  [the longest x1 43 us: local(): all_labels = lax.all_gather(best_class, ('cls', 'ptl'), axis=0, tiled=True)]
    pallas_call x0 -> x2, Pallas kernels: none -> 45.8 us  [the longest x1 24.8 us: local(): pl.pallas_call(functools.partial(spectra_kernel, groups, columns, step_pa...]
    reshape x2 -> x0, local copies, waits for them, and re-layouts: 26 us -> none  [the longest x1 14.6 us: local(): outgoing = outgoing.at[:, slot_index, :].set(aligned).reshape(freq_count,...]
    all_to_all x4 -> x0, local copies, waits for them, and re-layouts: 22.4 us -> none  [the longest x1 11.1 us: local(): lax.all_to_all(outgoing, 'cls', split_axis=1, concat_axis=1, tiled=True)]
    all_to_all x4 -> x0, starting transfers between devices: 21.4 us -> none  [the longest x1 6.51 us: local(): lax.all_to_all(labels, 'cls', split_axis=1, concat_axis=1, tiled=True)]
  transfers between devices with their start and end apart: 5 -> 3, of which waited for: 2 -> 2; matrix products, arithmetic and copies ran while one was open for 35% -> 2% of each run, Pallas kernels for 0% -> 14%
where the time goes in v1:
time: 151 us
  blocking collectives  59.8 us (40%)
  Pallas kernels  45.8 us (30%)
  waiting for transfers between devices  23.6 us (16%)
  between operations  13.8 us (9%)
  other arithmetic  4.65 us (3%)
  local copies, waits for them, and re-layouts  2.75 us (2%)
    all_gather x1, blocking collectives, local(): all_labels = lax.all_gather(best_class, ('cls', 'ptl'), axis=0, tiled=True)  43 us
    pallas_call x1, Pallas kernels, local(): pl.pallas_call(functools.partial(spectra_kernel, groups, columns, step_pa...  24.8 us
    all_gather x1, waiting for transfers between devices, local(): panels = lax.all_gather(panels, 'ptl', axis=1, tiled=True)  21.4 us
    pallas_call x1, Pallas kernels, local(): pl.pallas_call(functools.partial(score_kernel, groups), grid=(count_p //...  21 us
    all_gather x1, blocking collectives, local(): panels = lax.all_gather(own, 'cls', axis=0, tiled=True)  16.8 us
  transfers between devices with their start and end apart: 3, of which 2 were waited for; matrix products, arithmetic and copies ran while one was open for 2% of the time, Pallas kernels for 14%

profile of v1, /device:TPU:0, one launch (start us, length us, event | category | flops | bytes accessed | tf_op | source)
XLA Modules:
  0.0 150.5 jit_solution(8070610677757408415)
XLA Ops:
  7.2 0.0 reduce-scatter.3.cloned.1.call-start
  7.2 0.1 sine_negate_fusion
  7.4 1.5 %fusion.5 = (f32[19,512]{1,0:T(8,128)}, f32[19,512]{1,0:T(8,128)}) fusion(s32[512]{0:T(512)} %param.9), kind=kLoop, calls=%fused_computation.10 | loop fusion | flops 87552 | bytes 79872 | tf_op jit(solution)/shard_map/sin | solution.py:256
  8.9 0.6 fusion.11.table_ref
  9.5 0.0 copy-start
  9.5 24.8 %spectra.1 = (bf16[2,256,8192]{2,1,0:T(8,128)(2,1)}, bf16[64,200,128]{2,1,0:T(8,128)(2,1)}) custom-call(bf16[128,128]{1,0:T(8,128)(2,1)} %fusion.11.table_ref, bf16[512,64,128]{2,1,0:T(8,128)(2,1)} %high_ref.1, bf16[512,64,128]{2,1,0:T(8,128)(2,1)} %high_ref.1, s32[1,512]{1,0:T(1,128)} %bitcast.15, f32[19,512]{1,0:T(8,128)} %get-tuple-element.7.cos_ref, ...), custom_call_target="tpu_custom_call" | custom-call | flops 20000000000 | bytes 20000000 | tf_op jit(solution)/shard_map/spectra/pallas_call | solution.py:221
  34.3 0.0 copy-start.1
  34.3 0.0 reduce-scatter.3.cloned.1.call-update
  34.4 0.0 all-gather.4.cloned.1.call-start
  34.4 0.0 copy-done
  34.4 0.1 reshape.36
  34.5 16.8 %all-gather = bf16[4,50,1024]{2,1,0:T(8,128)(2,1)S(1)} all-gather(bf16[1,50,1024]{2,1,0:T(8,128)(2,1)S(1)} %reshape.36), channel_id=1, replica_groups=mesh['cls'=4,'ptl'=8] {'cls'}, dimensions={0}, use_global_device_ids=true | all-gather | bytes 512000 | tf_op jit(solution)/shard_map/all_gather | solution.py:205
  51.3 0.9 reshape.37
  52.2 0.0 all-gather.4.cloned.1.call-update
  52.2 0.0 reduce-scatter.5.cloned.1.call-start
  52.3 0.0 copy-done.1
  52.3 43.0 %all-gather.1 = s32[32,1,512]{2,1,0:T(1,128)S(1)} all-gather(s32[1,1,512]{2,1,0:T(1,128)S(1)} %bitcast.16), channel_id=1, replica_groups=mesh['cls'=4,'ptl'=8] {'cls','ptl'}, dimensions={0}, use_global_device_ids=true | all-gather | bytes 67584 | tf_op jit(solution)/shard_map/all_gather | solution.py:207
  95.2 0.7 convert_reduce_fusion
  95.9 0.0 reduce-scatter.3.cloned.1.call-done
  95.9 1.8 %copy.11 = bf16[8,200,128]{2,0,1:T(8,128)(2,1)} copy(bf16[8,200,128]{2,1,0:T(8,128)(2,1)} %reduce-scatter.3.cloned.1.call-done) | data formatting | bytes 819200 | tf_op jit(solution)/shard_map/reduce_scatter | solution.py:259
  97.7 0.0 reduce-scatter.5.cloned.1.call-update
  97.7 21.4 %all-gather.4.cloned.1.call-done.panels_ref = bf16[200,8192]{1,0:T(8,128)(2,1)} async-done(((bf16[200,1024]{1,0:T(8,128)(2,1)}), bf16[200,8192]{1,0:T(8,128)(2,1)}) %all-gather.4.cloned.1.call-update) | async-done | bytes 3276816 | tf_op jit(solution)/shard_map/all_gather | solution.py:206
  119.1 21.0 %score.1 = f32[1,512]{1,0:T(1,128)} custom-call(bf16[152,152]{1,0:T(8,128)(2,1)} %constant.47.clone.cos_ref, bf16[136,136]{1,0:T(8,128)(2,1)} %constant.48.clone.sin_ref, bf16[200,8192]{1,0:T(8,128)(2,1)} %all-gather.4.cloned.1.call-done.panels_ref, bf16[512,8192]{1,0:T(8,128)(2,1)} %bitcast.17), custom_call_target="tpu_custom_call" | custom-call | flops 20000000000 | bytes 20000000 | tf_op jit(solution)/shard_map/score/pallas_call | solution.py:273
  140.1 2.1 %reduce-scatter.5.cloned.1.call-done = bf16[8,1,50,128]{3,0,2,1:T(8,128)(2,1)} async-done(((bf16[8,4,50,128]{3,0,2,1:T(8,128)(2,1)}), bf16[8,1,50,128]{3,0,2,1:T(8,128)(2,1)}) %reduce-scatter.5.cloned.1.call-update) | async-done | bytes 102416 | tf_op jit(solution)/shard_map/reduce_scatter | solution.py:260
  142.3 1.7 %convert_divide_fusion = f32[8,50,128]{2,0,1:T(8,128)} fusion(bf16[8,1,50,128]{3,0,2,1:T(8,128)(2,1)} %reduce-scatter.5.cloned.1.call-done, f32[50]{0:T(128)S(1)} %broadcast_add_fusion), kind=kLoop, calls=%fused_computation.1 | loop fusion | flops 102400 | bytes 307400 | tf_op jit(solution)/shard_map/div | solution.py:300
  (2 shorter events, 0.0 us)
Async XLA Ops:
  7.2 88.7 %reduce-scatter.3.cloned.1.call-start = ((), (), s32[]{:S(2)}) async-start(), calls=%async_computation.3 | async-start | bytes 3686400 | tf_op jit(solution)/shard_map/reduce_scatter | solution.py:259
  9.5 24.9 %copy-start = (bf16[8,50,128]{2,0,1:T(8,128)(2,1)S(1)}, bf16[8,50,128]{2,0,1:T(8,128)(2,1)}, u32[]{:S(2)}) copy-start(bf16[8,50,128]{2,0,1:T(8,128)(2,1)} %param.7) | copy-start | bytes 307204
  34.3 17.9 %copy-start.1 = (s32[512]{0:T(512)S(1)}, s32[512]{0:T(512)}, u32[]{:S(2)}) copy-start(s32[512]{0:T(512)} %param.8) | copy-start | bytes 6148
  34.4 84.8 %all-gather.4.cloned.1.call-start = ((), (), s32[]{:S(2)}) async-start(), calls=%async_computation.2 | async-start | bytes 3686400 | tf_op jit(solution)/shard_map/all_gather | solution.py:206
  52.2 90.1 %reduce-scatter.5.cloned.1.call-start = ((), (), s32[]{:S(2)}) async-start(), calls=%async_computation.4 | async-start | bytes 512000 | tf_op jit(solution)/shard_map/reduce_scatter | solution.py:260
Sparse Core Ops, SparseCore 0:
  34.5 49.8 reduce-scatter.2
  86.2 32.8 all-gather.3
  121.4 20.8 reduce-scatter.4

commit v2 on v1

v2 whole, which is shorter than its diff:
```python
import functools
import math

import jax
import jax.numpy as jnp
import numpy as np
from jax import lax
from jax.experimental import pallas as pl
from jax.experimental.pallas import tpu as pltpu
from jax.sharding import PartitionSpec as P

ROTS = 36
LANES = 128
VMEM_LIMIT = 62 * 1024 * 1024
NT = (((1,), (1,)), ((), ()))


def fold_groups(freq_count, turns):
    groups = [[] for _ in range(turns // 2 + 1)]
    for m in range(freq_count):
        rest = m % turns
        if rest <= turns // 2:
            groups[rest].append((m, 1))
        else:
            groups[turns - rest].append((m, -1))
    return groups


def spectrum_table(angles, freq_count):
    position = jnp.arange(angles, dtype=jnp.int32)
    freq_index = jnp.arange(freq_count, dtype=jnp.int32)
    phases = (
        2.0
        * math.pi
        / angles
        * (position[:, None] * freq_index[None, :] % angles).astype(jnp.float32)
    )
    factor = 1.0 / math.sqrt(angles)
    return (jnp.concatenate([jnp.cos(phases), -jnp.sin(phases)], axis=1) * factor).astype(
        jnp.bfloat16
    )


def swap_halves(panel):
    half = panel.shape[-1] // 2
    return pltpu.roll(panel, half, panel.ndim - 1)


def flip_bit(index, bit):
    step = 1 << bit
    return index + step * (1 - 2 * ((index // step) % 2))


def subsets(bits):
    out = [()]
    for bit in bits:
        out = out + [taken + (bit,) for taken in out]
    return out


def flip_bits(index, bits):
    for bit in bits:
        index = flip_bit(index, bit)
    return index


def bit_count(size):
    return size.bit_length() - 1


def main_kernel(
    groups,
    columns,
    step_pairs,
    dft_steps,
    owners,
    peers,
    rows_used,
    block,
    table_ref,
    low_ref,
    high_ref,
    class_ref,
    cos_ref,
    sin_ref,
    cos_mat_ref,
    sin_mat_ref,
    own_ref,
    best_ref,
    totals_ref,
    counts_ref,
    raw_ref,
    held_ref,
    panels_ref,
    sums_ref,
    landed_ref,
    last_ref,
    stacked_ref,
    even_ref,
    odd_ref,
    gather_z_send,
    gather_z_recv,
    gather_send,
    gather_recv,
    scatter_send,
    scatter_recv,
    scatter_z_send,
    scatter_z_recv,
):
    step = pl.program_id(0)
    freq_count = len(columns)
    half = LANES // 2
    row_count = own_ref.shape[0]
    freqs_dev = freq_count // peers
    class_rows = owners * rows_used
    last = len(groups) - 1
    bits = bit_count(peers)
    me_z = lax.axis_index("cls")
    me = lax.axis_index("ptl")
    half_rows = [slice(0, row_count // 2), slice(row_count // 2, row_count)]
    down = list(range(bits))[::-1]
    up = list(range(bits))
    gather_orders = [down, [down[1], down[0]] + down[2:]]
    scatter_orders = [up, up[:-2] + [up[-1], up[-2]]]

    def gather_z_copies():
        return [
            pltpu.make_async_remote_copy(
                src_ref=own_ref,
                dst_ref=panels_ref.at[me, me_z],
                send_sem=gather_z_send.at[d - 1],
                recv_sem=gather_z_recv.at[d - 1],
                device_id=(lax.rem(me_z + d, owners), me),
                device_id_type=pl.DeviceIdType.MESH,
            )
            for d in range(1, owners)
        ]

    def gather_copies(phase):
        out = []
        for side, order in enumerate(gather_orders):
            partner = flip_bit(me, order[phase])
            for n, taken in enumerate(subsets(order[:phase])):
                part = panels_ref.at[flip_bits(me, taken), :, half_rows[side], :]
                out.append(
                    pltpu.make_async_remote_copy(
                        src_ref=part,
                        dst_ref=part,
                        send_sem=gather_send.at[side, (1 << phase) - 1 + n],
                        recv_sem=gather_recv.at[side, (1 << phase) - 1 + n],
                        device_id=(me_z, partner),
                        device_id_type=pl.DeviceIdType.MESH,
                    )
                )
        return out

    def scatter_slots(phase):
        return subsets(range(bits - 1 - phase)), sum(1 << (bits - 1 - k) for k in range(phase))

    def scatter_copies(phase):
        out = []
        for side, order in enumerate(scatter_orders):
            partner = flip_bit(me, order[phase])
            _, base = scatter_slots(phase)
            for n, taken in enumerate(subsets(order[phase + 1 :])):
                out.append(
                    pltpu.make_async_remote_copy(
                        src_ref=sums_ref.at[flip_bits(partner, taken), :, :, half_rows[side], :],
                        dst_ref=landed_ref.at[base + n, :, :, half_rows[side], :],
                        send_sem=scatter_send.at[side, base + n],
                        recv_sem=scatter_recv.at[side, base + n],
                        device_id=(me_z, partner),
                        device_id_type=pl.DeviceIdType.MESH,
                    )
                )
        return out

    def scatter_add(phase):
        for copy in scatter_copies(phase):
            copy.wait()
        _, base = scatter_slots(phase)
        for side, order in enumerate(scatter_orders):
            rows = half_rows[side]
            for n, taken in enumerate(subsets(order[phase + 1 :])):
                kept = flip_bits(me, taken)
                sums_ref[kept, :, :, rows, :] = (
                    sums_ref[kept, :, :, rows, :].astype(jnp.float32)
                    + landed_ref[base + n, :, :, rows, :].astype(jnp.float32)
                ).astype(jnp.bfloat16)

    def scatter_z_copies():
        out = []
        for d in range(1, owners):
            target = lax.rem(me_z + d, owners)
            out.append(
                pltpu.make_async_remote_copy(
                    src_ref=sums_ref.at[me, :, target],
                    dst_ref=last_ref.at[d - 1],
                    send_sem=scatter_z_send.at[d - 1],
                    recv_sem=scatter_z_recv.at[d - 1],
                    device_id=(target, me),
                    device_id_type=pl.DeviceIdType.MESH,
                )
            )
        return out

    @pl.when(step == 0)
    def _():
        barrier = pltpu.get_barrier_semaphore()
        for d in range(1, owners):
            pl.semaphore_signal(
                barrier,
                inc=1,
                device_id=(lax.rem(me_z + d, owners), me),
                device_id_type=pl.DeviceIdType.MESH,
            )
        for bit in range(bits):
            pl.semaphore_signal(
                barrier,
                inc=1,
                device_id=(me_z, flip_bit(me, bit)),
                device_id_type=pl.DeviceIdType.MESH,
            )
        pl.semaphore_wait(barrier, owners - 1 + bits)
        panels_ref[me, me_z] = own_ref[...]
        for copy in gather_z_copies():
            copy.start()

    gather_at = [dft_steps * (k + 1) // (bits + 1) + 1 for k in range(bits - 1)] + [dft_steps]
    for phase in range(bits):

        @pl.when(step == gather_at[phase])
        def _(phase=phase):
            for copy in gather_z_copies() if phase == 0 else gather_copies(phase - 1):
                copy.wait()
            for copy in gather_copies(phase):
                copy.start()

    @pl.when(step < dft_steps)
    def _():
        table = table_ref[...]
        together = 4

        def pair_step(at, carry):
            for k in range(together):
                pair = at * together + k
                rows = jnp.concatenate([low_ref[pair], high_ref[pair]], axis=0)
                raw_ref[pl.ds(pair, 2 * freq_count, stride=step_pairs), :] = lax.dot_general(
                    table, rows, NT, preferred_element_type=jnp.float32
                )
            return carry

        lax.fori_loop(0, step_pairs // together, pair_step, 0)
        first_half = lax.broadcasted_iota(jnp.int32, (step_pairs, LANES), 1) < half
        own_rows = pl.ds(pl.multiple_of(step * step_pairs, step_pairs), step_pairs)
        for m in range(freq_count):
            real = raw_ref[m * step_pairs : (m + 1) * step_pairs, :]
            imag = raw_ref[(freq_count + m) * step_pairs : (freq_count + m + 1) * step_pairs, :]
            at = slice(columns[m] * LANES, (columns[m] + 1) * LANES)
            held_ref[0, own_rows, at] = jnp.where(first_half, real, swap_halves(imag)).astype(
                jnp.bfloat16
            )
            held_ref[1, own_rows, at] = jnp.where(first_half, swap_halves(real), imag).astype(
                jnp.bfloat16
            )

    @pl.when(step == dft_steps)
    def _():
        count_p = class_ref.shape[1]
        half_p = count_p // 2
        member = lax.broadcasted_iota(jnp.int32, (class_rows, count_p), 0) == class_ref[...]
        lane = lax.broadcasted_iota(jnp.int32, (class_rows, LANES), 1)
        flip = jnp.where(lane < half, 1.0, -1.0)
        padding = jnp.zeros((row_count - rows_used, LANES), jnp.float32)
        column = 0
        for folded, group in enumerate(groups):
            at = slice(column, column + len(group) * LANES)
            column += len(group) * LANES
            weights = jnp.concatenate(
                [
                    jnp.where(member, cos_ref[folded : folded + 1, :], 0.0),
                    jnp.where(member, sin_ref[folded : folded + 1, :], 0.0),
                ],
                axis=0,
            ).astype(jnp.bfloat16)
            both = jnp.dot(
                weights[:, :half_p], held_ref[0, :, at], preferred_element_type=jnp.float32
            ) + jnp.dot(
                weights[:, half_p:], held_ref[1, :, at], preferred_element_type=jnp.float32
            )
            for place, (m, sign) in enumerate(group):
                part = both[:, place * LANES : (place + 1) * LANES]
                turned = swap_halves(part[class_rows:]) * flip
                total = part[:class_rows] + (turned if sign > 0 else -turned)
                for owner in range(owners):
                    sums_ref[m // freqs_dev, m % freqs_dev, owner] = jnp.concatenate(
                        [total[owner * rows_used : (owner + 1) * rows_used], padding], axis=0
                    ).astype(jnp.bfloat16)
        for copy in scatter_copies(0):
            copy.start()

    @pl.when(step == dft_steps + 1)
    def _():
        for copy in gather_copies(bits - 1):
            copy.wait()
        lane = lax.broadcasted_iota(jnp.int32, (rows_used, LANES), 1)
        flip = jnp.where(lane < half, 1.0, -1.0)
        for m in range(freq_count):
            sign = [s for group in groups for k, s in group if k == m][0]
            weight = 1.0 if m == 0 else 2.0
            at = slice(columns[m] * LANES, (columns[m] + 1) * LANES)
            source = slice(m % freqs_dev * LANES, (m % freqs_dev + 1) * LANES)
            for owner in range(owners):
                panel = panels_ref[m // freqs_dev, owner, :rows_used, source]
                panel = panel.astype(jnp.float32) * weight
                rows = slice(owner * rows_used, (owner + 1) * rows_used)
                stacked_ref[0, rows, at] = panel.astype(jnp.bfloat16)
                stacked_ref[1, rows, at] = (swap_halves(panel) * (flip * sign)).astype(
                    jnp.bfloat16
                )
        counts = jnp.zeros((row_count, LANES), jnp.float32)
        for peer in range(peers):
            for owner in range(owners):
                counts += panels_ref[peer, owner, :, freqs_dev * LANES :].astype(jnp.float32)
        counts_ref[...] = counts
        scatter_add(0)
        for copy in scatter_copies(1):
            copy.start()

    @pl.when(step >= dft_steps + 2)
    def _():
        tiles = class_rows // 8
        chunk = step - (dft_steps + 2)
        row = chunk * block
        half_p = held_ref.shape[1]
        rows = pl.ds(pl.multiple_of(row % half_p, block), block)
        column = 0
        for folded, group in enumerate(groups):
            at = slice(column, column + len(group) * LANES)
            column += len(group) * LANES
            taken = held_ref[row // half_p, rows, at]
            even = lax.dot_general(
                stacked_ref[0, :, at], taken, NT, preferred_element_type=jnp.float32
            )
            even_ref[:, folded * 8 : (folded + 1) * 8, :] = even.reshape(tiles, 8, -1)
            if 0 < folded < last:
                odd = lax.dot_general(
                    stacked_ref[1, :, at], taken, NT, preferred_element_type=jnp.float32
                )
                odd_ref[:, (folded - 1) * 8 : folded * 8, :] = odd.reshape(tiles, 8, -1)

        for phase in range(1, bits):

            @pl.when(chunk == min(phase - 1, 1))
            def _(phase=phase):
                scatter_add(phase)
                for copy in scatter_copies(phase + 1) if phase + 1 < bits else scatter_z_copies():
                    copy.start()

        cos_mat, sin_mat = cos_mat_ref[...], sin_mat_ref[...]

        def tile_step(tile, best):
            even = jnp.dot(
                cos_mat, even_ref[tile].astype(jnp.bfloat16), preferred_element_type=jnp.float32
            )
            odd = jnp.dot(
                sin_mat, odd_ref[tile].astype(jnp.bfloat16), preferred_element_type=jnp.float32
            )
            best = jnp.maximum(best, jnp.maximum(even[:8], even[last * 8 :]))
            for turn in range(1, last):
                best = jnp.maximum(
                    best,
                    even[turn * 8 : (turn + 1) * 8] + jnp.abs(odd[(turn - 1) * 8 : turn * 8]),
                )
            return best

        best = lax.fori_loop(0, tiles, tile_step, jnp.full((8, block), -jnp.inf, jnp.float32))
        best_ref[0] = jnp.max(best, axis=0, keepdims=True)

        @pl.when(step == pl.num_programs(0) - 1)
        def _():
            for copy in scatter_z_copies():
                copy.wait()
            total = sums_ref[me, :, me_z].astype(jnp.float32)
            for d in range(1, owners):
                total += last_ref[d - 1].astype(jnp.float32)
            totals_ref[...] = total


def local(particles, references, best_class, best_turn):
    count_p, cycle_count, angles = particles.shape
    freq_count = angles // 2
    groups = fold_groups(freq_count, ROTS)
    last = len(groups) - 1
    columns = [0] * freq_count
    place = 0
    for group in groups:
        for m, _ in group:
            columns[m] = place
            place += 1
    owners, peers = lax.axis_size("cls"), lax.axis_size("ptl")
    bits = bit_count(peers)
    freqs_dev, classes_dev, _ = references.shape
    rows_used = -(-classes_dev // 8) * 8
    row_count = -(-classes_dev // 32) * 32
    class_rows = owners * rows_used

    own = jnp.transpose(references, (1, 0, 2)).reshape(classes_dev, freqs_dev * LANES)
    own = jnp.concatenate([own, own[: row_count - classes_dev]], axis=0)
    owner_of = best_class // classes_dev
    local_class = best_class - owner_of * classes_dev
    row_of = jnp.where(
        jnp.arange(LANES, dtype=jnp.int32)[None, :] == owner_of[:, None], local_class[:, None], -1
    )
    own_counts = jnp.sum(
        (
            row_of[:, None, :owners] == jnp.arange(row_count, dtype=jnp.int32)[None, :, None]
        ).astype(jnp.float32),
        axis=0,
    )
    own_counts = jnp.pad(own_counts, ((0, 0), (0, LANES - owners)))
    own = jnp.concatenate([own, own_counts.astype(jnp.bfloat16)], axis=1)

    step_pairs = 32
    pairs = count_p // 2
    dft_steps = pairs // step_pairs
    folded_index = jnp.arange(last + 1, dtype=jnp.int32)
    phases = (
        2.0
        * math.pi
        / ROTS
        * (folded_index[:, None] * best_turn[None, :] % ROTS).astype(jnp.float32)
    )
    table = spectrum_table(angles, freq_count).T
    turn_index = np.arange(last + 1)
    turn_phase = 2.0 * math.pi / ROTS * (turn_index[:, None] * turn_index[None, :] % ROTS)
    spread = np.eye(8, dtype=np.float32)
    cos_mat = jnp.asarray(np.kron(np.cos(turn_phase).astype(np.float32), spread), jnp.bfloat16)
    sin_mat = jnp.asarray(
        np.kron(-np.sin(turn_phase[1:last, 1:last]).astype(np.float32), spread), jnp.bfloat16
    )
    block = min(256 if class_rows <= 256 else 128, pairs)
    chunks = count_p // block
    whole = lambda *_: (0, 0)
    best_score, totals, counts = pl.pallas_call(
        functools.partial(
            main_kernel,
            groups,
            columns,
            step_pairs,
            dft_steps,
            owners,
            peers,
            rows_used,
            block,
        ),
        grid=(dft_steps + 2 + chunks,),
        out_shape=(
            jax.ShapeDtypeStruct((chunks, 1, block), jnp.float32),
            jax.ShapeDtypeStruct((freqs_dev, row_count, LANES), jnp.float32),
            jax.ShapeDtypeStruct((row_count, LANES), jnp.float32),
        ),
        in_specs=[
            pl.BlockSpec((angles, 2 * freq_count), whole),
            pl.BlockSpec(
                (step_pairs, cycle_count, angles),
                lambda g: (jnp.minimum(g, dft_steps - 1), 0, 0),
            ),
            pl.BlockSpec(
                (step_pairs, cycle_count, angles),
                lambda g: (jnp.minimum(g, dft_steps - 1) + dft_steps, 0, 0),
            ),
            pl.BlockSpec((1, count_p), whole),
            pl.BlockSpec((last + 1, count_p), whole),
            pl.BlockSpec((last + 1, count_p), whole),
            pl.BlockSpec(cos_mat.shape, whole),
            pl.BlockSpec(sin_mat.shape, whole),
            pl.BlockSpec(memory_space=pltpu.VMEM),
        ],
        out_specs=(
            pl.BlockSpec((1, 1, block), lambda g: (jnp.maximum(g - dft_steps - 2, 0), 0, 0)),
            pl.BlockSpec(memory_space=pltpu.VMEM),
            pl.BlockSpec(memory_space=pltpu.VMEM),
        ),
        scratch_shapes=[
            pltpu.VMEM((2 * freq_count * step_pairs, LANES), jnp.float32),
            pltpu.VMEM((2, pairs, freq_count * LANES), jnp.bfloat16),
            pltpu.VMEM((peers, owners, row_count, (freqs_dev + 1) * LANES), jnp.bfloat16),
            pltpu.VMEM((peers, freqs_dev, owners, row_count, LANES), jnp.bfloat16),
            pltpu.VMEM((peers - 1, freqs_dev, owners, row_count, LANES), jnp.bfloat16),
            pltpu.VMEM((owners - 1, freqs_dev, row_count, LANES), jnp.bfloat16),
            pltpu.VMEM((2, class_rows, freq_count * LANES), jnp.bfloat16),
            pltpu.VMEM((class_rows // 8, 8 * (last + 1), block), jnp.float32),
            pltpu.VMEM((class_rows // 8, 8 * (last - 1), block), jnp.float32),
            pltpu.SemaphoreType.DMA((owners - 1,)),
            pltpu.SemaphoreType.DMA((owners - 1,)),
            pltpu.SemaphoreType.DMA((2, peers - 1)),
            pltpu.SemaphoreType.DMA((2, peers - 1)),
            pltpu.SemaphoreType.DMA((2, peers - 1)),
            pltpu.SemaphoreType.DMA((2, peers - 1)),
            pltpu.SemaphoreType.DMA((owners - 1,)),
            pltpu.SemaphoreType.DMA((owners - 1,)),
        ],
        compiler_params=pltpu.CompilerParams(
            vmem_limit_bytes=VMEM_LIMIT, collective_id=0, has_side_effects=True
        ),
        name="classify",
    )(
        table,
        particles,
        particles,
        (owner_of * rows_used + local_class).reshape(1, count_p),
        jnp.cos(phases),
        jnp.sin(phases),
        cos_mat,
        sin_mat,
        own,
    )
    my_counts = lax.dynamic_slice_in_dim(counts, lax.axis_index("cls"), 1, axis=1)
    new_references = totals[:, :classes_dev] / (my_counts[None, :classes_dev] + 1.0)
    return (best_score.reshape(count_p), new_references)


def solution(mesh):
    return jax.shard_map(
        local,
        mesh=mesh,
        in_specs=(
            P(("cls", "ptl"), None, None),
            P("ptl", "cls", None),
            P(("cls", "ptl")),
            P(("cls", "ptl")),
        ),
        out_specs=(P(("cls", "ptl")), P("ptl", "cls", None)),
        check_vma=False,
    )
```

time: 151 us -> 96.2 us (0.64)
  blocking collectives: 59.8 us -> 0 us
  Pallas kernels: 45.8 us -> 83.9 us
  waiting for transfers between devices: 23.6 us -> 0 us
  between operations: 13.8 us -> 0.67 us
  other arithmetic: 4.65 us -> 7.06 us
    all_gather x2 -> x0, blocking collectives: 59.8 us -> none  [the longest x1 43 us: local(): all_labels = lax.all_gather(best_class, ('cls', 'ptl'), axis=0, tiled=True)]
    pallas_call x2 -> x1, Pallas kernels: 45.8 us -> 83.9 us  [local(): pl.pallas_call(functools.partial(main_kernel, groups, columns, step_pairs...]
    all_gather x1 -> x0, waiting for transfers between devices: 21.4 us -> none  [local(): panels = lax.all_gather(panels, 'ptl', axis=1, tiled=True)]
    add x2, other arithmetic: 0.01 us -> 2.19 us  [the longest x1 1.26 us: local(): owner_of * rows_used + local_class]
    reduce_scatter x2 -> x0, waiting for transfers between devices: 2.16 us -> none  [the longest x1 2.14 us: local(): lax.psum_scatter(totals.reshape(freqs_dev, owners, classes_dev, LANES), '...]
    unnamed x6, local copies, waits for them, and re-layouts: 0.95 us -> 2.92 us
    reduce_scatter x1 -> x0, local copies, waits for them, and re-layouts: 1.8 us -> none  [local(): totals = lax.psum_scatter(sums, 'ptl', scatter_dimension=0, tiled=True)]
  transfers between devices with their start and end apart: 3 -> 0, of which waited for: 2 -> 0; matrix products, arithmetic and copies ran while one was open for 2% -> 0% of each run, Pallas kernels for 14% -> 0%
where the time goes in v2:
time: 96.2 us; the launch traced here: 95.4 us
  Pallas kernels  83.9 us (87%)
  other arithmetic  7.06 us (7%)
  local copies, waits for them, and re-layouts  3.79 us (4%)
    pallas_call x1, Pallas kernels, local(): pl.pallas_call(functools.partial(main_kernel, groups, columns, step_pairs...  83.9 us
    unnamed x6, local copies, waits for them, and re-layouts  2.92 us

profile of v2, /device:TPU:0, one launch (start us, length us, event | category | flops | bytes accessed | tf_op | source)
XLA Modules:
  0.0 95.4 jit_solution(847737961706730270)
XLA Ops:
  0.6 0.7 multiply_subtract_fusion
  1.3 0.1 convert_reduce_fusion
  1.5 0.1 copy.12
  1.6 0.9 pad.12
  2.5 0.8 slice.20
  3.3 0.7 fusion.1.own_ref
  4.0 0.1 sine_negate_fusion
  4.1 0.6 fusion.13.table_ref
  4.7 1.3 %multiply_add_fusion = s32[512]{0:T(512)} fusion(s32[512]{0:T(512)S(1)} %get-tuple-element.17, s32[512]{0:T(512)} %param.8), kind=kLoop, calls=%fused_computation.35 | loop fusion | flops 2048 | bytes 6144 | tf_op jit(solution)/shard_map/add | solution.py:512
  6.0 1.5 %fusion.7 = (f32[19,512]{1,0:T(8,128)}, f32[19,512]{1,0:T(8,128)}) fusion(s32[512]{0:T(512)} %param.9), kind=kLoop, calls=%fused_computation.14 | loop fusion | flops 87552 | bytes 79872 | tf_op jit(solution)/shard_map/sin | solution.py:514
  7.6 83.9 %classify.1 = (f32[2,1,256]{2,1,0:T(1,128)}, f32[8,64,128]{2,1,0:T(8,128)}, f32[64,128]{1,0:T(8,128)}) custom-call(bf16[128,128]{1,0:T(8,128)(2,1)} %fusion.13.table_ref, bf16[512,64,128]{2,1,0:T(8,128)(2,1)} %high_ref.1, bf16[512,64,128]{2,1,0:T(8,128)(2,1)} %high_ref.1, s32[1,512]{1,0:T(1,128)} %bitcast.17, f32[19,512]{1,0:T(8,128)} %get-tuple-element.19.cos_ref, ...), custom_call_target="tpu_custom_call" | custom-call | tf_op jit(solution)/shard_map/classify/pallas_call | solution.py:445
  91.5 0.9 fusion.17
  92.4 1.0 %slice_divide_fusion = f32[8,50,128]{2,1,0:T(8,128)S(1)} fusion(f32[8,64,128]{2,1,0:T(8,128)} %get-tuple-element.6, f32[50]{0:T(128)S(1)} %fusion.17), kind=kLoop, calls=%fused_computation.4 | loop fusion | flops 51200 | bytes 409800 | tf_op jit(solution)/shard_map/div | solution.py:520
  93.4 0.7 copy.13
  94.2 1.3 %copy.17 = f32[512]{0:T(512)} copy(f32[512]{0:T(512)} %bitcast.18) | data formatting | bytes 4096
  (4 shorter events, 0.0 us)

commit v3 on v2

--- a/solution.py
+++ b/solution.py
@@ -24,21 +24,6 @@
         else:
             groups[turns - rest].append((m, -1))
     return groups
-
-
-def spectrum_table(angles, freq_count):
-    position = jnp.arange(angles, dtype=jnp.int32)
-    freq_index = jnp.arange(freq_count, dtype=jnp.int32)
-    phases = (
-        2.0
-        * math.pi
-        / angles
-        * (position[:, None] * freq_index[None, :] % angles).astype(jnp.float32)
-    )
-    factor = 1.0 / math.sqrt(angles)
-    return (jnp.concatenate([jnp.cos(phases), -jnp.sin(phases)], axis=1) * factor).astype(
-        jnp.bfloat16
-    )
 
 
 def swap_halves(panel):
@@ -81,8 +66,8 @@
     low_ref,
     high_ref,
     class_ref,
-    cos_ref,
-    sin_ref,
+    turn_ref,
+    turn_table_ref,
     cos_mat_ref,
     sin_mat_ref,
     own_ref,
@@ -110,14 +95,15 @@
     step = pl.program_id(0)
     freq_count = len(columns)
     half = LANES // 2
-    row_count = own_ref.shape[0]
     freqs_dev = freq_count // peers
+    own_rows, sum_rows = own_ref.shape[0], freqs_dev * rows_used
     class_rows = owners * rows_used
     last = len(groups) - 1
     bits = bit_count(peers)
     me_z = lax.axis_index("cls")
     me = lax.axis_index("ptl")
-    half_rows = [slice(0, row_count // 2), slice(row_count // 2, row_count)]
+    gather_rows = [slice(0, own_rows // 2), slice(own_rows // 2, own_rows)]
+    half_rows = [slice(0, sum_rows // 2), slice(sum_rows // 2, sum_rows)]
     down = list(range(bits))[::-1]
     up = list(range(bits))
     gather_orders = [down, [down[1], down[0]] + down[2:]]
@@ -141,7 +127,7 @@
         for side, order in enumerate(gather_orders):
             partner = flip_bit(me, order[phase])
             for n, taken in enumerate(subsets(order[:phase])):
-                part = panels_ref.at[flip_bits(me, taken), :, half_rows[side], :]
+                part = panels_ref.at[flip_bits(me, taken), :, gather_rows[side], :]
                 out.append(
                     pltpu.make_async_remote_copy(
                         src_ref=part,
@@ -165,8 +151,8 @@
             for n, taken in enumerate(subsets(order[phase + 1 :])):
                 out.append(
                     pltpu.make_async_remote_copy(
-                        src_ref=sums_ref.at[flip_bits(partner, taken), :, :, half_rows[side], :],
-                        dst_ref=landed_ref.at[base + n, :, :, half_rows[side], :],
+                        src_ref=sums_ref.at[flip_bits(partner, taken), :, half_rows[side], :],
+                        dst_ref=landed_ref.at[base + n, :, half_rows[side], :],
                         send_sem=scatter_send.at[side, base + n],
                         recv_sem=scatter_recv.at[side, base + n],
                         device_id=(me_z, partner),
@@ -183,9 +169,9 @@
             rows = half_rows[side]
             for n, taken in enumerate(subsets(order[phase + 1 :])):
                 kept = flip_bits(me, taken)
-                sums_ref[kept, :, :, rows, :] = (
-                    sums_ref[kept, :, :, rows, :].astype(jnp.float32)
-                    + landed_ref[base + n, :, :, rows, :].astype(jnp.float32)
+                sums_ref[kept, :, rows, :] = (
+                    sums_ref[kept, :, rows, :].astype(jnp.float32)
+                    + landed_ref[base + n, :, rows, :].astype(jnp.float32)
                 ).astype(jnp.bfloat16)
 
     def scatter_z_copies():
@@ -194,7 +180,7 @@
             target = lax.rem(me_z + d, owners)
             out.append(
                 pltpu.make_async_remote_copy(
-                    src_ref=sums_ref.at[me, :, target],
+                    src_ref=sums_ref.at[me, target],
                     dst_ref=last_ref.at[d - 1],
                     send_sem=scatter_z_send.at[d - 1],
                     recv_sem=scatter_z_recv.at[d - 1],
@@ -226,7 +212,7 @@
         for copy in gather_z_copies():
             copy.start()
 
-    gather_at = [dft_steps * (k + 1) // (bits + 1) + 1 for k in range(bits - 1)] + [dft_steps]
+    gather_at = [dft_steps * (k + 1) // bits + 1 for k in range(bits - 1)] + [dft_steps + 1]
     for phase in range(bits):
 
         @pl.when(step == gather_at[phase])
@@ -239,23 +225,18 @@
     @pl.when(step < dft_steps)
     def _():
         table = table_ref[...]
-        together = 4
-
-        def pair_step(at, carry):
-            for k in range(together):
-                pair = at * together + k
-                rows = jnp.concatenate([low_ref[pair], high_ref[pair]], axis=0)
-                raw_ref[pl.ds(pair, 2 * freq_count, stride=step_pairs), :] = lax.dot_general(
-                    table, rows, NT, preferred_element_type=jnp.float32
-                )
-            return carry
-
-        lax.fori_loop(0, step_pairs // together, pair_step, 0)
+        for start in range(0, step_pairs, 8):
+            rows = jnp.concatenate(
+                [ref[start + k] for k in range(8) for ref in (low_ref, high_ref)], axis=0
+            )
+            raw = lax.dot_general(table, rows, NT, preferred_element_type=jnp.float32)
+            raw = jnp.stack([raw[:, k * LANES : (k + 1) * LANES] for k in range(8)], axis=0)
+            raw_ref[:, start : start + 8, :] = jnp.swapaxes(raw, 0, 1)
         first_half = lax.broadcasted_iota(jnp.int32, (step_pairs, LANES), 1) < half
         own_rows = pl.ds(pl.multiple_of(step * step_pairs, step_pairs), step_pairs)
         for m in range(freq_count):
-            real = raw_ref[m * step_pairs : (m + 1) * step_pairs, :]
-            imag = raw_ref[(freq_count + m) * step_pairs : (freq_count + m + 1) * step_pairs, :]
+            real = raw_ref[m]
+            imag = raw_ref[freq_count + m]
             at = slice(columns[m] * LANES, (columns[m] + 1) * LANES)
             held_ref[0, own_rows, at] = jnp.where(first_half, real, swap_halves(imag)).astype(
                 jnp.bfloat16
@@ -269,17 +250,21 @@
         count_p = class_ref.shape[1]
         half_p = count_p // 2
         member = lax.broadcasted_iota(jnp.int32, (class_rows, count_p), 0) == class_ref[...]
+        turns = turn_table_ref.shape[2]
+        at_turn = lax.broadcasted_iota(jnp.int32, (turns, count_p), 0) == turn_ref[...]
+        at_turn = jnp.where(at_turn, 1.0, 0.0).astype(jnp.bfloat16)
+        cosines = jnp.dot(turn_table_ref[0], at_turn, preferred_element_type=jnp.float32)
+        sines = jnp.dot(turn_table_ref[1], at_turn, preferred_element_type=jnp.float32)
         lane = lax.broadcasted_iota(jnp.int32, (class_rows, LANES), 1)
         flip = jnp.where(lane < half, 1.0, -1.0)
-        padding = jnp.zeros((row_count - rows_used, LANES), jnp.float32)
         column = 0
         for folded, group in enumerate(groups):
             at = slice(column, column + len(group) * LANES)
             column += len(group) * LANES
             weights = jnp.concatenate(
                 [
-                    jnp.where(member, cos_ref[folded : folded + 1, :], 0.0),
-                    jnp.where(member, sin_ref[folded : folded + 1, :], 0.0),
+                    jnp.where(member, cosines[folded : folded + 1, :], 0.0),
+                    jnp.where(member, sines[folded : folded + 1, :], 0.0),
                 ],
                 axis=0,
             ).astype(jnp.bfloat16)
@@ -293,14 +278,18 @@
                 turned = swap_halves(part[class_rows:]) * flip
                 total = part[:class_rows] + (turned if sign > 0 else -turned)
                 for owner in range(owners):
-                    sums_ref[m // freqs_dev, m % freqs_dev, owner] = jnp.concatenate(
-                        [total[owner * rows_used : (owner + 1) * rows_used], padding], axis=0
-                    ).astype(jnp.bfloat16)
+                    row = m % freqs_dev * rows_used
+                    sums_ref[m // freqs_dev, owner, row : row + rows_used, :] = total[
+                        owner * rows_used : (owner + 1) * rows_used
+                    ].astype(jnp.bfloat16)
         for copy in scatter_copies(0):
             copy.start()
 
     @pl.when(step == dft_steps + 1)
     def _():
+        scatter_add(0)
+        for copy in scatter_copies(1):
+            copy.start()
         for copy in gather_copies(bits - 1):
             copy.wait()
         lane = lax.broadcasted_iota(jnp.int32, (rows_used, LANES), 1)
@@ -309,23 +298,20 @@
             sign = [s for group in groups for k, s in group if k == m][0]
             weight = 1.0 if m == 0 else 2.0
             at = slice(columns[m] * LANES, (columns[m] + 1) * LANES)
-            source = slice(m % freqs_dev * LANES, (m % freqs_dev + 1) * LANES)
+            source = slice(m % freqs_dev * rows_used, (m % freqs_dev + 1) * rows_used)
             for owner in range(owners):
-                panel = panels_ref[m // freqs_dev, owner, :rows_used, source]
+                panel = panels_ref[m // freqs_dev, owner, source, :]
                 panel = panel.astype(jnp.float32) * weight
                 rows = slice(owner * rows_used, (owner + 1) * rows_used)
                 stacked_ref[0, rows, at] = panel.astype(jnp.bfloat16)
                 stacked_ref[1, rows, at] = (swap_halves(panel) * (flip * sign)).astype(
                     jnp.bfloat16
                 )
-        counts = jnp.zeros((row_count, LANES), jnp.float32)
+        counts = jnp.zeros(counts_ref.shape, jnp.float32)
         for peer in range(peers):
             for owner in range(owners):
-                counts += panels_ref[peer, owner, :, freqs_dev * LANES :].astype(jnp.float32)
+                counts += panels_ref[peer, owner, sum_rows:, :].astype(jnp.float32)
         counts_ref[...] = counts
-        scatter_add(0)
-        for copy in scatter_copies(1):
-            copy.start()
 
     @pl.when(step >= dft_steps + 2)
     def _():
@@ -334,8 +320,20 @@
         row = chunk * block
         half_p = held_ref.shape[1]
         rows = pl.ds(pl.multiple_of(row % half_p, block), block)
+
+        def reduce_further(at_chunk, phases):
+            @pl.when(chunk == at_chunk)
+            def _():
+                for phase in phases:
+                    scatter_add(phase)
+                    more = scatter_copies(phase + 1) if phase + 1 < bits else scatter_z_copies()
+                    for copy in more:
+                        copy.start()
+
         column = 0
         for folded, group in enumerate(groups):
+            if folded == len(groups) // 3:
+                reduce_further(1, range(2, bits))
             at = slice(column, column + len(group) * LANES)
             column += len(group) * LANES
             taken = held_ref[row // half_p, rows, at]
@@ -349,14 +347,7 @@
                 )
                 odd_ref[:, (folded - 1) * 8 : folded * 8, :] = odd.reshape(tiles, 8, -1)
 
-        for phase in range(1, bits):
-
-            @pl.when(chunk == min(phase - 1, 1))
-            def _(phase=phase):
-                scatter_add(phase)
-                for copy in scatter_copies(phase + 1) if phase + 1 < bits else scatter_z_copies():
-                    copy.start()
-
+        reduce_further(0, range(1, 2))
         cos_mat, sin_mat = cos_mat_ref[...], sin_mat_ref[...]
 
         def tile_step(tile, best):
@@ -381,7 +372,7 @@
         def _():
             for copy in scatter_z_copies():
                 copy.wait()
-            total = sums_ref[me, :, me_z].astype(jnp.float32)
+            total = sums_ref[me, me_z].astype(jnp.float32)
             for d in range(1, owners):
                 total += last_ref[d - 1].astype(jnp.float32)
             totals_ref[...] = total
@@ -402,11 +393,10 @@
     bits = bit_count(peers)
     freqs_dev, classes_dev, _ = references.shape
     rows_used = -(-classes_dev // 8) * 8
-    row_count = -(-classes_dev // 32) * 32
+    sum_rows = freqs_dev * rows_used
+    row_count = -(-(sum_rows + classes_dev) // 32) * 32 - sum_rows
     class_rows = owners * rows_used
 
-    own = jnp.transpose(references, (1, 0, 2)).reshape(classes_dev, freqs_dev * LANES)
-    own = jnp.concatenate([own, own[: row_count - classes_dev]], axis=0)
     owner_of = best_class // classes_dev
     local_class = best_class - owner_of * classes_dev
     row_of = jnp.where(
@@ -419,19 +409,22 @@
         axis=0,
     )
     own_counts = jnp.pad(own_counts, ((0, 0), (0, LANES - owners)))
-    own = jnp.concatenate([own, own_counts.astype(jnp.bfloat16)], axis=1)
+    padded = jnp.concatenate([references, references[:, : rows_used - classes_dev]], axis=1)
+    own = jnp.concatenate(
+        [padded.reshape(freqs_dev * rows_used, LANES), own_counts.astype(jnp.bfloat16)], axis=0
+    )
 
     step_pairs = 32
     pairs = count_p // 2
     dft_steps = pairs // step_pairs
-    folded_index = jnp.arange(last + 1, dtype=jnp.int32)
-    phases = (
-        2.0
-        * math.pi
-        / ROTS
-        * (folded_index[:, None] * best_turn[None, :] % ROTS).astype(jnp.float32)
-    )
-    table = spectrum_table(angles, freq_count).T
+    angle = 2.0 * math.pi / angles * (np.outer(np.arange(freq_count), np.arange(angles)) % angles)
+    table = np.concatenate([np.cos(angle), -np.sin(angle)], axis=0) / math.sqrt(angles)
+    table = jnp.asarray(table.astype(np.float32), jnp.bfloat16)
+    turn = 2.0 * math.pi / ROTS * (np.outer(np.arange(last + 1), np.arange(ROTS)) % ROTS)
+    turn_table = np.zeros((2, -(-(last + 1) // 16) * 16, -(-ROTS // 16) * 16), np.float32)
+    turn_table[0, : last + 1, :ROTS] = np.cos(turn)
+    turn_table[1, : last + 1, :ROTS] = np.sin(turn)
+    turn_table = jnp.asarray(turn_table, jnp.bfloat16)
     turn_index = np.arange(last + 1)
     turn_phase = 2.0 * math.pi / ROTS * (turn_index[:, None] * turn_index[None, :] % ROTS)
     spread = np.eye(8, dtype=np.float32)
@@ -457,7 +450,7 @@
         grid=(dft_steps + 2 + chunks,),
         out_shape=(
             jax.ShapeDtypeStruct((chunks, 1, block), jnp.float32),
-            jax.ShapeDtypeStruct((freqs_dev, row_count, LANES), jnp.float32),
+            jax.ShapeDtypeStruct((sum_rows, LANES), jnp.float32),
             jax.ShapeDtypeStruct((row_count, LANES), jnp.float32),
         ),
         in_specs=[
@@ -471,8 +464,8 @@
                 lambda g: (jnp.minimum(g, dft_steps - 1) + dft_steps, 0, 0),
             ),
             pl.BlockSpec((1, count_p), whole),
-            pl.BlockSpec((last + 1, count_p), whole),
-            pl.BlockSpec((last + 1, count_p), whole),
+            pl.BlockSpec((1, count_p), whole),
+            pl.BlockSpec(turn_table.shape, lambda g: (0, 0, 0)),
             pl.BlockSpec(cos_mat.shape, whole),
             pl.BlockSpec(sin_mat.shape, whole),
             pl.BlockSpec(memory_space=pltpu.VMEM),
@@ -483,12 +476,12 @@
             pl.BlockSpec(memory_space=pltpu.VMEM),
         ),
         scratch_shapes=[
-            pltpu.VMEM((2 * freq_count * step_pairs, LANES), jnp.float32),
+            pltpu.VMEM((2 * freq_count, step_pairs, LANES), jnp.float32),
             pltpu.VMEM((2, pairs, freq_count * LANES), jnp.bfloat16),
-            pltpu.VMEM((peers, owners, row_count, (freqs_dev + 1) * LANES), jnp.bfloat16),
-            pltpu.VMEM((peers, freqs_dev, owners, row_count, LANES), jnp.bfloat16),
-            pltpu.VMEM((peers - 1, freqs_dev, owners, row_count, LANES), jnp.bfloat16),
-            pltpu.VMEM((owners - 1, freqs_dev, row_count, LANES), jnp.bfloat16),
+            pltpu.VMEM((peers, owners, sum_rows + row_count, LANES), jnp.bfloat16),
+            pltpu.VMEM((peers, owners, sum_rows, LANES), jnp.bfloat16),
+            pltpu.VMEM((peers - 1, owners, sum_rows, LANES), jnp.bfloat16),
+            pltpu.VMEM((owners - 1, sum_rows, LANES), jnp.bfloat16),
             pltpu.VMEM((2, class_rows, freq_count * LANES), jnp.bfloat16),
             pltpu.VMEM((class_rows // 8, 8 * (last + 1), block), jnp.float32),
             pltpu.VMEM((class_rows // 8, 8 * (last - 1), block), jnp.float32),
@@ -510,13 +503,14 @@
         particles,
         particles,
         (owner_of * rows_used + local_class).reshape(1, count_p),
-        jnp.cos(phases),
-        jnp.sin(phases),
+        best_turn.reshape(1, count_p),
+        turn_table,
         cos_mat,
         sin_mat,
         own,
     )
     my_counts = lax.dynamic_slice_in_dim(counts, lax.axis_index("cls"), 1, axis=1)
+    totals = totals.reshape(freqs_dev, rows_used, LANES)
     new_references = totals[:, :classes_dev] / (my_counts[None, :classes_dev] + 1.0)
     return (best_score.reshape(count_p), new_references)
 

time: 96.2 us -> 77 us (0.80)
  Pallas kernels: 83.9 us -> 67.4 us
  local copies, waits for them, and re-layouts: 3.79 us -> 2.08 us
    pallas_call x1, Pallas kernels: 83.9 us -> 67.4 us  [local(): pl.pallas_call(functools.partial(main_kernel, groups, columns, step_pairs...]
    unnamed x6 -> x1, local copies, waits for them, and re-layouts: 2.92 us -> 1.24 us
    sin x1 -> x0, other arithmetic: 1.54 us -> none  [local(): jnp.sin(phases)]
where the time goes in v3:
time: 77 us; the launch traced here: 76.5 us
  Pallas kernels  67.4 us (88%)
  other arithmetic  6.36 us (8%)
  local copies, waits for them, and re-layouts  2.08 us (3%)
    pallas_call x1, Pallas kernels, local(): pl.pallas_call(functools.partial(main_kernel, groups, columns, step_pairs...  67.4 us
    div x1, other arithmetic, local(): totals[:, :classes_dev] / (my_counts[None, :classes_dev] + 1.0)  1.75 us

profile of v3, /device:TPU:0, one launch (start us, length us, event | category | flops | bytes accessed | tf_op | source)
XLA Modules:
  0.0 76.5 jit_solution(10317717503603126493)
XLA Ops:
  0.6 0.7 multiply_subtract_fusion
  1.3 1.3 %multiply_add_fusion = s32[512]{0:T(512)} fusion(s32[512]{0:T(512)S(1)} %get-tuple-element.9, s32[512]{0:T(512)} %param.10), kind=kLoop, calls=%fused_computation.13 | loop fusion | flops 2048 | bytes 6144 | tf_op jit(solution)/shard_map/add | solution.py:505
  2.6 0.1 convert_reduce_fusion
  2.7 0.7 slice.12
  3.4 0.1 copy.18
  3.6 0.9 %pad_maximum_fusion = bf16[8,56,128]{2,0,1:T(8,128)(2,1)S(1)} fusion(bf16[8,6,128]{2,0,1:T(8,128)(2,1)S(1)} %slice.12, bf16[8,50,128]{2,0,1:T(8,128)(2,1)} %param.9), kind=kLoop, calls=%fused_computation.6 | loop fusion | flops 57344 | bytes 229376 | tf_op jit(solution)/shard_map/concatenate | solution.py:412
  4.5 0.7 fusion.1.own_ref
  5.2 67.4 %classify.1 = (f32[2,1,256]{2,1,0:T(1,128)}, f32[448,128]{1,0:T(8,128)}, f32[64,128]{1,0:T(8,128)}) custom-call(bf16[128,128]{1,0:T(8,128)(2,1)} %constant.38.clone.table_ref, bf16[512,64,128]{2,1,0:T(8,128)(2,1)} %high_ref.1, bf16[512,64,128]{2,1,0:T(8,128)(2,1)} %high_ref.1, s32[1,512]{1,0:T(1,128)} %bitcast.8, s32[1,512]{1,0:T(1,128)} %bitcast.9, ...), custom_call_target="tpu_custom_call" | custom-call | tf_op jit(solution)/shard_map/classify/pallas_call | solution.py:438
  72.6 0.9 %fusion.2 = f32[50]{0:T(128)S(1)} fusion(f32[64,128]{1,0:T(8,128)} %get-tuple-element.7, s32[]{:T(128)S(6)} %select_n.14), kind=kLoop, calls=%fused_computation.8 | loop fusion | flops 50 | bytes 404 | tf_op jit(solution)/shard_map/add | solution.py:514
  73.5 1.8 %copy_divide_fusion = f32[8,50,128]{2,0,1:T(8,128)} fusion(f32[8,50,128]{2,1,0:T(8,128)} %bitcast.7, f32[50]{0:T(128)S(1)} %fusion.2), kind=kLoop, calls=%fused_computation.4 | loop fusion | flops 51200 | bytes 409800 | tf_op jit(solution)/shard_map/div | solution.py:514
  75.3 1.2 %copy.23 = f32[512]{0:T(512)} copy(f32[512]{0:T(512)} %bitcast.10) | data formatting | bytes 4096
  (2 shorter events, 0.0 us)
